TPU v7x, 32 devices: a whole 2x2x4 slice. The times are simulated.
32 devices in a mesh: group: 8 (over z, y), head: 4 (over x, core).
Axes of the slice: x: 2, y: 2, z: 4, core: 2. Of those that a mesh axis runs over, the one named last changes fastest.
Arguments:
- queries: bfloat16 [2048, 3072], P('group', 'head'), may hold values from -160 to 160, as said below
- keys_new: bfloat16 [2048, 3072], P('group', 'head'), may hold values from -7 to 7, as said below
- values_new: bfloat16 [2048, 3072], P('group', 'head'), may hold values from -6 to 6
- cache_keys: bfloat16 [512, 3072], P('group', 'head'), may hold values from -6 to 6
- cache_values: bfloat16 [512, 3072], P('group', 'head'), may hold values from -6 to 6
- valid_rows: int32 [8], replicated, may hold values from 32 to 64
- finished: int32 [8], replicated, may hold values from 5 to 8
- levels: int32 [8], P('group'), may hold values from 0 to 63
- gate_table: float32 [64, 6144], P(None, 'head'), may hold values from 0.5 to 4
- out_weight: bfloat16 [3072, 6144], P(None, 'head'), may hold values from -1.75 to 1.75
- latents: bfloat16 [48, 256, 512], P('group', 'head'), may hold values from -6 to 6
- conv_weight: bfloat16 [3, 512, 512], replicated, may hold values from -0.15625 to 0.15625
Outputs:
- mixed: bfloat16 [2048, 6144], P('group', 'head')
- decoded: bfloat16 [48, 256, 512], P('group', 'head')
Inputs may be any that keep to these rules, and one draw needn't show every extreme that they name: `queries`: normal entries, with some rows made large multiples of keys in some draws. `keys_new`: normal entries.
All inputs are finite; a program needn't handle non-finite values.
Results may differ from a plain program's by a relative error of at most 0.01.
Values may be sent and summed in bfloat16 or wider, within the bound.
A program may use at most 128 MiB of HBM per device.

v0:
```python
import jax
import jax.numpy as jnp
from jax import lax
from jax.sharding import PartitionSpec as P

HD = 128
KROWS = 64


NEGATIVE = -1e30


def shifted(array, axis, by):
    length = lax.axis_size(axis)
    pairs = [(i, i + by) for i in range(length) if 0 <= i + by < length]
    return lax.ppermute(array, axis, pairs)


def attend(carried, key_rows, value_rows, usable, query_heads):
    top_old, total_old, summed_old = carried
    heads_local = query_heads.shape[1]
    key_heads = key_rows.reshape(-1, heads_local, HD)
    value_heads = value_rows.reshape(-1, heads_local, HD)
    scores = jnp.einsum(
        "qhd,khd->hqk", query_heads, key_heads, preferred_element_type=jnp.float32
    ) * HD ** (-0.5)
    scores = jnp.where(usable[None, None, :], scores, NEGATIVE)
    top_new = jnp.maximum(top_old, jnp.max(scores, axis=-1))
    rescale = jnp.exp(top_old - top_new)
    weights = jnp.where(usable[None, None, :], jnp.exp(scores - top_new[..., None]), 0.0)
    total_new = total_old * rescale + jnp.sum(weights, axis=-1)
    update = jnp.einsum(
        "hqk,khd->hqd",
        weights.astype(jnp.bfloat16),
        value_heads,
        preferred_element_type=jnp.float32,
    )
    return (top_new, total_new, summed_old * rescale[..., None] + update)


def shards(
    queries,
    keys_new,
    values_new,
    cache_keys,
    cache_values,
    valid_rows,
    finished,
    levels,
    gate_table,
    out_weight,
    latents,
    conv_weight,
):
    heads_local = queries.shape[1] // HD
    query_rows = queries.shape[0]
    query_heads = queries.reshape(query_rows, heads_local, HD)
    group_total = valid_rows.shape[0]
    group_ids = jnp.arange(group_total, dtype=jnp.int32)
    my_group = lax.axis_index("group")
    my_limit = jnp.sum(jnp.where(group_ids == my_group, finished, 0))

    def usable_rows(first, number):
        global_rows = first + jnp.arange(number, dtype=jnp.int32)
        owner = global_rows // KROWS
        offset = global_rows % KROWS
        matches = owner[:, None] == group_ids[None, :]
        limits = jnp.sum(jnp.where(matches, valid_rows[None, :], 0), axis=1)
        return (owner < my_limit) & (offset < limits)

    initial = (
        jnp.full((heads_local, query_rows), NEGATIVE, jnp.float32),
        jnp.zeros((heads_local, query_rows), jnp.float32),
        jnp.zeros((heads_local, query_rows, HD), jnp.float32),
    )
    initial = attend(
        initial, keys_new, values_new, jnp.ones((keys_new.shape[0],), dtype=bool), query_heads
    )

    def fold_cache(carried, pieces, first):
        key_piece, value_piece = pieces
        number = key_piece.shape[0]
        width = 512
        blocks = number // width
        if blocks == 1:
            return attend(carried, key_piece, value_piece, usable_rows(first, number), query_heads)

        def one_block(inner, index):
            begin = index * width
            key_block = lax.dynamic_slice_in_dim(key_piece, begin, width, 0)
            value_block = lax.dynamic_slice_in_dim(value_piece, begin, width, 0)
            return (
                attend(
                    inner, key_block, value_block, usable_rows(first + begin, width), query_heads
                ),
                None,
            )

        return lax.scan(one_block, carried, jnp.arange(blocks, dtype=jnp.int32))[0]

    top_all, total_all, summed_all = fold_cache(
        initial,
        (
            lax.all_gather(cache_keys, "group", axis=0, tiled=True),
            lax.all_gather(cache_values, "group", axis=0, tiled=True),
        ),
        jnp.int32(0),
    )
    attended = summed_all / total_all[..., None]
    attended = (
        jnp.transpose(attended, (1, 0, 2))
        .reshape(query_rows, heads_local * HD)
        .astype(jnp.bfloat16)
    )
    attended_all = lax.all_gather(attended, "head", axis=1, tiled=True)
    projected = jnp.dot(attended_all, out_weight, preferred_element_type=jnp.float32)
    selector = (jnp.arange(gate_table.shape[0], dtype=jnp.int32) == levels[0]).astype(jnp.float32)[
        None, :
    ]
    gate_row = jnp.dot(selector, gate_table, precision=lax.Precision.HIGHEST)
    mixed = (projected * gate_row).astype(jnp.bfloat16)
    frames = latents.shape[0]
    previous = shifted(latents[frames - 2 :], "group", 1)
    extended = jnp.concatenate([previous, latents], axis=0)
    decoded = jnp.zeros(latents.shape, jnp.float32)
    for k in range(3):
        decoded = decoded + jnp.einsum(
            "tpc,cd->tpd",
            extended[2 - k : 2 - k + frames],
            conv_weight[k],
            preferred_element_type=jnp.float32,
        )
    return (mixed, decoded.astype(jnp.bfloat16))


def solution(mesh):
    in_specs = (
        P("group", "head"),
        P("group", "head"),
        P("group", "head"),
        P("group", "head"),
        P("group", "head"),
        P(),
        P(),
        P("group"),
        P(None, "head"),
        P(None, "head"),
        P("group", "head", None),
        P(),
    )
    out_specs = (P("group", "head"), P("group", "head", None))
    return jax.shard_map(shards, mesh=mesh, in_specs=in_specs, out_specs=out_specs, check_vma=False)
```

profile of v0, /device:TPU:1, one launch (start us, length us, event | category | flops | bytes accessed | tf_op | source)
XLA Modules:
  0.0 119.4 jit_solution(13617921738910978943)
XLA Ops:
  7.2 0.0 copy-start
  7.2 0.0 copy-start.6
  7.2 0.0 copy-start.4
  7.2 0.0 all-gather.2.cloned.1.call-start
  7.3 0.0 copy-start.7
  7.3 0.0 copy-start.8
  7.3 28.5 %all_gather.10 = bf16[512,768]{1,0:T(8,128)(2,1)S(1)} all-gather(bf16[64,768]{1,0:T(8,128)(2,1)} %param.16), channel_id=1, replica_groups=mesh['group'=8,'head'=4] {'group'}, dimensions={0}, use_global_device_ids=true | all-gather | bytes 884736 | tf_op jit(solution)/shard_map/all_gather | solution.py:105
  35.8 1.2 copy.49
  36.9 1.2 copy.40
  38.1 0.0 copy-done.6
  38.1 27.1 %all_gather.9 = bf16[512,768]{1,0:T(8,128)(2,1)S(1)} all-gather(bf16[64,768]{1,0:T(8,128)(2,1)S(1)} %copy-done.6), channel_id=1, replica_groups=mesh['group'=8,'head'=4] {'group'}, dimensions={0}, use_global_device_ids=true | all-gather | bytes 884736 | tf_op jit(solution)/shard_map/all_gather | solution.py:104
  65.2 0.3 copy.46
  65.5 0.0 copy-done.4
  65.5 0.2 copy.41
  65.6 0.0 copy-done.7
  65.7 0.1 select_reduce_fusion
  65.7 0.0 copy-done.8
  65.7 0.6 fusion.41
  66.4 0.7 compare_and_fusion
  67.0 0.4 fusion.49
  67.5 0.0 copy-start.3
  67.5 0.7 fusion
  68.2 0.9 fusion.2
  69.1 0.0 copy-done.3
  69.1 0.0 copy-start.5
  69.1 1.8 %fusion.9 = f32[256,6,128]{0,2,1:T(8,128)} fusion(bf16[512,6,128]{0,2,1:T(8,128)(2,1)S(1)} %bitcast.74, f32[6,256,512]{2,1,0:T(8,128)S(1)} %get-tuple-element.10, f32[6,256]{1,0:T(8,128)S(1)} %get-tuple-element.6, pred[512]{0:T(512)(128)(4,1)S(1)} %compare_and_fusion), kind=kOutput, calls=%fused_computation.14 | convolution fusion | flops 205258752 | bytes 4725248 | tf_op jit(solution)/shard_map/hqk,khd->hqd/dot_general | solution.py:32
  71.0 0.0 copy-done.5
  71.0 0.2 copy.44
  71.1 0.0 copy-start.1
  71.1 0.2 fusion.7
  71.4 2.3 %fusion.17 = bf16[256,6,128]{0,2,1:T(8,128)(2,1)} fusion(f32[256,6,128]{0,2,1:T(8,128)} %fusion.9, bf16[256,6,128]{0,2,1:T(8,128)(2,1)S(1)} %bitcast.76, f32[6,256,256]{1,2,0:T(8,128)S(1)} %get-tuple-element.8, f32[6,256]{1,0:T(8,128)S(1)} %get-tuple-element.5, f32[256,6]{0,1:T(8,128)S(1)} %get-tuple-element.2, f32[256,6]{0,1:T(8,128)S(1)} %get-tuple-element.3, ...), kind=kOutput, calls=%fused_computation.22 | convolution fusion | flops 102432768 | bytes 3170304 | tf_op jit(solution)/shard_map/hqk,khd->hqd/dot_general | solution.py:32
  73.7 0.0 copy-start.2
  73.7 0.0 all-gather.2.cloned.1.call-update
  73.7 0.0 copy-done.1
  73.8 1.4 %collective-permute-start = (bf16[2,64,512]{2,1,0:T(8,128)(2,1)S(1)}, bf16[2,64,512]{2,1,0:T(8,128)(2,1)S(1)}, u32[]{:S(2)}, u32[]{:S(2)}) collective-permute-start(bf16[2,64,512]{2,1,0:T(8,128)(2,1)S(1)} %slice.19), channel_id=1, source_target_pairs={{0,4},{4,8},{8,12},{12,16},{16,20},{20,24},{24,28},{1,5},{5,9},{9,... | collective-permute-start | bytes 393224 | tf_op jit(solution)/shard_map/ppermute | solution.py:16
  75.2 1.4 %fusion.22 = f32[6,64,512]{2,1,0:T(8,128)S(1)} fusion(bf16[6,64,512]{2,1,0:T(8,128)(2,1)S(1)} %copy-done.1, bf16[3,512,512]{2,1,0:T(8,128)(2,1)} %param.23), kind=kOutput, calls=%fused_computation.27 | convolution fusion | flops 201326592 | bytes 1703936 | tf_op jit(solution)/shard_map/tpc,cd->tpd/dot_general | solution.py:127
  77.3 0.0 copy-done
  77.3 0.3 convolution_reduce_fusion
  77.5 0.0 collective-permute-done
  77.6 0.0 copy-done.2
  77.6 0.4 convolution_add_fusion.1
  78.0 1.1 fusion.16
  79.1 25.8 %all-gather.2.cloned.1.call-done = bf16[256,3072]{0,1:T(8,128)(2,1)} async-done(((bf16[256,768]{0,1:T(8,128)(2,1)}), bf16[256,3072]{0,1:T(8,128)(2,1)}) %all-gather.2.cloned.1.call-update) | async-done | bytes 1572880 | tf_op jit(solution)/shard_map/all_gather | solution.py:115
  104.9 7.7 %fusion.1 = bf16[256,1536]{1,0:T(8,128)(2,1)} fusion(bf16[256,3072]{0,1:T(8,128)(2,1)} %all-gather.2.cloned.1.call-done, bf16[3072,1536]{1,0:T(8,128)(2,1)} %param.21, f32[1536]{0:T(1024)S(1)} %convolution_reduce_fusion), kind=kOutput, calls=%fused_computation.4 | convolution fusion | flops 2416705536 | bytes 11802624 | tf_op jit(solution)/shard_map/dot_general | solution.py:116
  (6 shorter events, 0.1 us)
Async XLA Ops:
  7.2 70.1 %copy-start = (f32[64,1536]{1,0:T(8,128)S(1)}, f32[64,1536]{1,0:T(8,128)}, u32[]{:S(2)}) copy-start(f32[64,1536]{1,0:T(8,128)} %param.20) | copy-start | bytes 1179652
  7.2 30.9 %copy-start.6 = (bf16[64,768]{1,0:T(8,128)(2,1)S(1)}, bf16[64,768]{1,0:T(8,128)(2,1)}, u32[]{:S(2)}) copy-start(bf16[64,768]{1,0:T(8,128)(2,1)} %param.15) | copy-start | bytes 294916
  7.2 58.3 %copy-start.4 = (bf16[256,768]{1,0:T(8,128)(2,1)S(1)}, bf16[256,768]{1,0:T(8,128)(2,1)}, u32[]{:S(2)}) copy-start(bf16[256,768]{1,0:T(8,128)(2,1)} %param.13) | copy-start | bytes 1179652
  7.2 97.7 %all-gather.2.cloned.1.call-start = ((), (), s32[]{:S(2)}) async-start(), calls=%async_computation | async-start | bytes 1966080 | tf_op jit(solution)/shard_map/all_gather | solution.py:115
  7.3 58.4 %copy-start.7 = (s32[8]{0:T(128)S(1)}, s32[8]{0:T(128)}, u32[]{:S(2)}) copy-start(s32[8]{0:T(128)} %param.17) | copy-start | bytes 100
  7.3 58.5 %copy-start.8 = (s32[8]{0:T(128)S(1)}, s32[8]{0:T(128)}, u32[]{:S(2)}) copy-start(s32[8]{0:T(128)} %param.18) | copy-start | bytes 100
  67.5 1.6 %copy-start.3 = (bf16[512,768]{0,1:T(8,128)(2,1)S(1)}, bf16[512,768]{0,1:T(8,128)(2,1)}, u32[]{:S(2)}) copy-start(bf16[512,768]{0,1:T(8,128)(2,1)} %copy.49) | copy-start | bytes 2359300
  69.1 1.8 %copy-start.5 = (bf16[256,768]{1,0:T(8,128)(2,1)S(1)}, bf16[256,768]{1,0:T(8,128)(2,1)}, u32[]{:S(2)}) copy-start(bf16[256,768]{1,0:T(8,128)(2,1)} %param.14) | copy-start | bytes 1179652
  71.1 2.6 %copy-start.1 = (bf16[6,64,512]{2,1,0:T(8,128)(2,1)S(1)}, bf16[6,64,512]{2,1,0:T(8,128)(2,1)}, u32[]{:S(2)}) copy-start(bf16[6,64,512]{2,1,0:T(8,128)(2,1)} %param.22) | copy-start | bytes 1179652
  73.7 3.9 %copy-start.2 = (bf16[3,512,512]{2,1,0:T(8,128)(2,1)S(1)}, bf16[3,512,512]{2,1,0:T(8,128)(2,1)}, u32[]{:S(2)}) copy-start(bf16[3,512,512]{2,1,0:T(8,128)(2,1)} %param.23) | copy-start | bytes 4718596
  73.8 3.8 %collective-permute-start = (bf16[2,64,512]{2,1,0:T(8,128)(2,1)S(1)}, bf16[2,64,512]{2,1,0:T(8,128)(2,1)S(1)}, u32[]{:S(2)}, u32[]{:S(2)}) collective-permute-start(bf16[2,64,512]{2,1,0:T(8,128)(2,1)S(1)} %slice.19), channel_id=1, source_target_pairs={{0,4},{4,8},{8,12},{12,16},{16,20},{20,24},{24,28},{1,5},{5,9},{9,... | collective-permute-start | bytes 393224 | tf_op jit(solution)/shard_map/ppermute | solution.py:16
Sparse Core Ops, SparseCore 0:
  73.8 30.9 all-gather.1
where the time goes:
time: 120 us; the launch traced here: 119 us
  blocking collectives  55.6 us (46%)
  waiting for transfers between devices  25.8 us (22%)
  matrix products  16.1 us (13%)
  between operations  14.9 us (12%)
  local copies, waits for them, and re-layouts  3.04 us (3%)
  other arithmetic  2.52 us (2%)
  starting transfers between devices  1.47 us (1%)
    all_gather x1, blocking collectives, shards(): lax.all_gather(cache_values, 'group', axis=0, tiled=True)  28.5 us
    all_gather x1, blocking collectives, shards(): lax.all_gather(cache_keys, 'group', axis=0, tiled=True)  27.1 us
    all_gather x1, waiting for transfers between devices, shards(): attended_all = lax.all_gather(attended, 'head', axis=1, tiled=True)  25.8 us
    dot_general x1, matrix products, shards(): jnp.dot(attended_all, out_weight, preferred_element_type=jnp.float32)  7.66 us
    dot_general x2, matrix products, attend(): jnp.einsum('hqk,khd->hqd', weights.astype(jnp.bfloat16), value_heads, pre...  4.12 us
    dot_general x3, matrix products, shards(): jnp.einsum('tpc,cd->tpd', extended[2 - k:2 - k + frames], conv_weight[k],...  2.89 us
  transfers between devices with their start and end apart: 2, of which 1 were waited for; matrix products, arithmetic and copies ran while one was open for 3% of the time, Pallas kernels for 0%

commit v1 on v0

v1 whole, which is shorter than its diff:
```python
import functools

import jax
import jax.numpy as jnp
from jax import lax
from jax.experimental import pallas as pl
from jax.experimental.pallas import tpu as pltpu
from jax.sharding import PartitionSpec as P

HD = 128
NEGATIVE = -1e30
LOG2E = 1.4426950408889634
MESH = pl.DeviceIdType.MESH
NT = (((1,), (1,)), ((), ()))


def kernel(
    cfg,
    q_hbm, kn_hbm, vn_hbm, ck_hbm, cv_hbm,
    valid_ref, finished_ref, level_ref,
    gate_hbm, w_hbm, lat_hbm, cw_hbm,
    mixed_ref, dec_ref,
    kv, q, kn, vn, att, w, gate, ext, cw, acc, bias,
    kv_load, w_load, load, kv_recv, up_send, down_send, y_send,
    att_recv, att_send, halo_send, halo_recv,
):
    groups, pieces, per, ahead, crossing = cfg
    lines = groups // 2
    krows = kv.shape[4]
    heads_local = pieces * per
    n_head = att.shape[1]
    wide = per * HD
    pix = ext.shape[0] - lat_hbm.shape[0]
    rows = lat_hbm.shape[0]

    g = lax.axis_index("group")
    hd = lax.axis_index("head")
    z, y = g // 2, g % 2
    has_up, has_down = z < lines - 1, z > 0
    y_peer = z * 2 + 1 - y
    core_peer = (hd // 2) * 2 + 1 - hd % 2
    x_peer = (hd + 2) % n_head

    kv_copies = []
    for h in range(heads_local):
        for i, src in enumerate((ck_hbm, cv_hbm)):
            kv_copies.append(pltpu.make_async_copy(
                src.at[:, pl.ds(h * HD, HD)], kv.at[h // per, g, h % per, i], kv_load.at[2 * h + i]))
    for c in kv_copies:
        c.start()
    lat_copy = pltpu.make_async_copy(lat_hbm, ext.at[pl.ds(pix, rows)], load.at[0])
    cw_copy = pltpu.make_async_copy(cw_hbm, cw, load.at[1])
    q_copy = pltpu.make_async_copy(q_hbm, q, load.at[2])
    kn_copy = pltpu.make_async_copy(kn_hbm, kn, load.at[3])
    vn_copy = pltpu.make_async_copy(vn_hbm, vn, load.at[4])
    gate_copy = pltpu.make_async_copy(gate_hbm, gate, load.at[5])
    for c in (lat_copy, cw_copy, q_copy, kn_copy, vn_copy):
        c.start()

    barrier = pltpu.get_barrier_semaphore()

    def greet(group, head):
        pl.semaphore_signal(barrier, inc=1, device_id={"group": group, "head": head}, device_id_type=MESH)

    greet(y_peer, hd)
    greet(g, core_peer)
    greet(g, x_peer)
    diag = jnp.where(y == 0, g - 1, g + 1)
    has_diag = jnp.where(y == 0, has_down, has_up)

    @pl.when(has_up)
    def _():
        greet(g + 2, hd)

    @pl.when(has_down)
    def _():
        greet(g - 2, hd)

    @pl.when(has_diag)
    def _():
        greet(diag, hd)

    pl.semaphore_wait(
        barrier, 3 + has_up.astype(jnp.int32) + has_down.astype(jnp.int32) + has_diag.astype(jnp.int32))

    def send_up(p, s):
        return pltpu.make_async_remote_copy(
            kv.at[p, s], kv.at[p, s], up_send.at[p, s], kv_recv.at[p, s],
            device_id={"group": g + 2, "head": hd}, device_id_type=MESH)

    def send_down(p, s):
        return pltpu.make_async_remote_copy(
            kv.at[p, s], kv.at[p, s], down_send.at[p, s], kv_recv.at[p, s],
            device_id={"group": g - 2, "head": hd}, device_id_type=MESH)

    def send_y(p, s):
        return pltpu.make_async_remote_copy(
            kv.at[p, s], kv.at[p, s], y_send.at[p, s // 2], kv_recv.at[p, s],
            device_id={"group": y_peer, "head": hd}, device_id_type=MESH)

    def received(p, s):
        send_y(p, s).wait_recv()

    def both_ways(p, s):
        @pl.when(has_up)
        def _():
            send_up(p, s).start()

        @pl.when(has_down)
        def _():
            send_down(p, s).start()

    def own_sends(p):
        for h in range(p * per, p * per + per):
            kv_copies[2 * h].wait()
            kv_copies[2 * h + 1].wait()
        if p in crossing:
            send_y(p, g).start()
            both_ways(p, g)
        else:
            both_ways(p, g)
            send_y(p, g).start()

    def forward(p):
        cross = p in crossing
        columns = (y, 1 - y) if cross else (y,)
        if cross:
            received(p, y_peer)
            both_ways(p, y_peer)

        def step(t, _):
            for col in columns:
                @pl.when(z >= t)
                def _():
                    s = (z - t) * 2 + col
                    received(p, s)

                    @pl.when(has_up)
                    def _():
                        send_up(p, s).start()

                    if not cross:
                        send_y(p, s).start()

                @pl.when(z + t < lines)
                def _():
                    s = (z + t) * 2 + col
                    received(p, s)

                    @pl.when(has_down)
                    def _():
                        send_down(p, s).start()

                    if not cross:
                        send_y(p, s).start()
            return 0

        lax.fori_loop(1, lines, step, 0)
        if not cross:
            def side(s, _):
                received(p, s * 2 + 1 - y)
                return 0

            lax.fori_loop(0, lines, side, 0)

    def finish_sends(p):
        cross = p in crossing

        def one(s, _):
            for col in ((0, 1) if cross else (y,)):
                @pl.when(has_up & (s <= z))
                def _():
                    send_up(p, s * 2 + col).wait_send()

                @pl.when(has_down & (s >= z))
                def _():
                    send_down(p, s * 2 + col).wait_send()
            if not cross:
                send_y(p, s * 2 + y).wait_send()
            return 0

        lax.fori_loop(0, lines, one, 0)
        if cross:
            send_y(p, g).wait_send()

    def att_copy(p, slot, which, peer):
        return pltpu.make_async_remote_copy(
            att.at[p, slot], att.at[p, slot], att_send.at[p, which], att_recv.at[p, slot],
            device_id={"group": g, "head": peer}, device_id_type=MESH)

    def attend(p):
        block_groups = min(groups, 8)
        width = block_groups * krows
        for j in range(per):
            h = p * per + j
            cols = pl.ds(h * HD, HD)
            qh = q[:, cols]

            def cached(b, i):
                return kv[p, b * block_groups:(b + 1) * block_groups, j, i].reshape(width, HD)

            def scores(b):
                s = lax.dot_general(qh, cached(b, 0), NT, preferred_element_type=jnp.float32)
                return s * (HD ** -0.5 * LOG2E) + bias[:, b * width:(b + 1) * width]

            own = lax.dot_general(qh, kn[:, cols], NT, preferred_element_type=jnp.float32) * (HD ** -0.5 * LOG2E)
            first = scores(0)
            top = jnp.maximum(jnp.max(own, axis=1, keepdims=True), jnp.max(first, axis=1, keepdims=True))
            w_own = jnp.exp2(own - top)
            w_first = jnp.exp2(first - top)
            total = jnp.sum(w_own, axis=1, keepdims=True) + jnp.sum(w_first, axis=1, keepdims=True)
            summed = jnp.dot(w_own.astype(jnp.bfloat16), vn[:, cols], preferred_element_type=jnp.float32)
            summed += jnp.dot(w_first.astype(jnp.bfloat16), cached(0, 1), preferred_element_type=jnp.float32)
            for b in range(1, groups // block_groups):
                s = scores(b)
                new = jnp.maximum(top, jnp.max(s, axis=1, keepdims=True))
                rescale = jnp.exp2(top - new)
                wb = jnp.exp2(s - new)
                total = total * rescale + jnp.sum(wb, axis=1, keepdims=True)
                summed = summed * rescale + jnp.dot(
                    wb.astype(jnp.bfloat16), cached(b, 1), preferred_element_type=jnp.float32)
                top = new
            att[p, hd, :, pl.ds(j * HD, HD)] = (summed / total).astype(jnp.bfloat16)
        att_copy(p, hd, 1, x_peer).start()
        att_copy(p, hd, 0, core_peer).start()

    def relay(p):
        att_copy(p, x_peer, 2, core_peer).wait_recv()
        att_copy(p, x_peer, 2, core_peer).start()

    def project(p):
        other = (core_peer + 2) % n_head
        att_copy(p, core_peer, 0, core_peer).wait_recv()
        att_copy(p, other, 0, core_peer).wait_recv()
        for c in w_copies[p]:
            c.wait()
        rows_in = jnp.concatenate([att[p, i] for i in range(n_head)], axis=1)
        tile = 512
        for n in range(0, acc.shape[1], tile):
            part = jnp.dot(rows_in, w[p, :, n:n + tile], preferred_element_type=jnp.float32)
            if p > 0:
                part = part + acc[:, n:n + tile]
            if p < pieces - 1:
                acc[:, n:n + tile] = part
            else:
                row = gate[pl.ds(level_ref[0], 1), n:n + tile]
                mixed_ref[:, n:n + tile] = (part * row).astype(jnp.bfloat16)

    def convolve(first, number):
        at = [ext[pix + first - k * (pix // 2): pix + first - k * (pix // 2) + number, :] for k in range(3)]
        total = jnp.dot(at[0], cw[0], preferred_element_type=jnp.float32)
        total += jnp.dot(at[1], cw[1], preferred_element_type=jnp.float32)
        total += jnp.dot(at[2], cw[2], preferred_element_type=jnp.float32)
        dec_ref[first:first + number, :] = total.astype(jnp.bfloat16)

    halo = pltpu.make_async_remote_copy(
        ext.at[pl.ds(rows, pix)], ext.at[pl.ds(0, pix)], halo_send, halo_recv,
        device_id={"group": g + 1, "head": hd}, device_id_type=MESH)

    for p in range(min(ahead, pieces)):
        own_sends(p)

    w_copies = []
    for p in range(pieces):
        w_copies.append([
            pltpu.make_async_copy(
                w_hbm.at[pl.ds((i * heads_local + p * per) * HD, wide)],
                w.at[p, pl.ds(i * wide, wide)], w_load.at[p, i])
            for i in range(n_head)])
        for c in w_copies[-1]:
            c.start()
    gate_copy.start()

    position = lax.broadcasted_iota(jnp.int32, (1, groups * krows), 1)
    owner, offset = position // krows, position % krows
    limit = jnp.zeros((1, groups * krows), jnp.int32)
    for j in range(groups):
        limit = jnp.where(owner == j, valid_ref[j], limit)
    usable = (owner < finished_ref[g]) & (offset < limit)
    bias[...] = jnp.where(usable, 0.0, NEGATIVE)

    @pl.when(g == 0)
    def _():
        ext[0:pix, :] = jnp.zeros((pix, ext.shape[1]), ext.dtype)

    lat_copy.wait()
    cw_copy.wait()
    convolve(pix, rows - pix)
    q_copy.wait()
    kn_copy.wait()
    vn_copy.wait()

    for p in range(pieces):
        if p + ahead < pieces:
            own_sends(p + ahead)
        forward(p)
        if p == pieces - 1:
            @pl.when(g < groups - 1)
            def _():
                halo.start()
        attend(p)
        if p >= 1:
            relay(p - 1)
        if p >= 2:
            project(p - 2)

    gate_copy.wait()
    if pieces >= 2:
        project(pieces - 2)

    @pl.when(g > 0)
    def _():
        halo.wait_recv()

    relay(pieces - 1)
    convolve(0, pix)
    project(pieces - 1)

    @pl.when(g < groups - 1)
    def _():
        halo.wait_send()

    for p in range(pieces):
        finish_sends(p)
        att_copy(p, hd, 1, x_peer).wait_send()
        att_copy(p, hd, 0, core_peer).wait_send()
        att_copy(p, x_peer, 2, core_peer).wait_send()


def shards(
    groups, n_head,
    queries, keys_new, values_new, cache_keys, cache_values,
    valid_rows, finished, levels, gate_table, out_weight, latents, conv_weight,
):
    qrows, width = queries.shape
    krows = cache_keys.shape[0]
    heads_local = width // HD
    features = out_weight.shape[1]
    frames, pixels, channels = latents.shape
    pieces = heads_local if groups <= 8 else 1
    per = heads_local // pieces
    crossing = (0,) if pieces > 1 else ()
    cfg = (groups, pieces, per, 2, crossing)
    lines = groups // 2
    bf16, f32 = jnp.bfloat16, jnp.float32
    dma = pltpu.SemaphoreType.DMA
    hbm = pl.BlockSpec(memory_space=pl.ANY)
    smem = pl.BlockSpec(memory_space=pltpu.SMEM)
    vmem = pl.BlockSpec(memory_space=pltpu.VMEM)
    mixed, decoded = pl.pallas_call(
        functools.partial(kernel, cfg),
        out_shape=(
            jax.ShapeDtypeStruct((qrows, features), bf16),
            jax.ShapeDtypeStruct((frames * pixels, channels), bf16),
        ),
        in_specs=[hbm] * 5 + [smem] * 3 + [hbm] * 4,
        out_specs=(vmem, vmem),
        scratch_shapes=[
            pltpu.VMEM((pieces, groups, per, 2, krows, HD), bf16),
            pltpu.VMEM((qrows, width), bf16),
            pltpu.VMEM((qrows, width), bf16),
            pltpu.VMEM((qrows, width), bf16),
            pltpu.VMEM((pieces, n_head, qrows, per * HD), bf16),
            pltpu.VMEM((pieces, n_head * per * HD, features), bf16),
            pltpu.VMEM(gate_table.shape, f32),
            pltpu.VMEM(((frames + 2) * pixels, channels), bf16),
            pltpu.VMEM(conv_weight.shape, bf16),
            pltpu.VMEM((qrows, features), f32),
            pltpu.VMEM((1, groups * krows), f32),
            dma((2 * heads_local,)),
            dma((pieces, n_head)),
            dma((6,)),
            dma((pieces, groups)),
            dma((pieces, groups)),
            dma((pieces, groups)),
            dma((pieces, lines)),
            dma((pieces, n_head)),
            dma((pieces, 3)),
            dma,
            dma,
        ],
        compiler_params=pltpu.CompilerParams(
            collective_id=0, has_side_effects=True, vmem_limit_bytes=56 * 2**20),
        name="video_attention",
    )(
        queries, keys_new, values_new, cache_keys, cache_values,
        valid_rows, finished, levels, gate_table, out_weight,
        latents.reshape(frames * pixels, channels), conv_weight,
    )
    return mixed, decoded.reshape(frames, pixels, channels)


def solution(mesh):
    in_specs = (
        P("group", "head"),
        P("group", "head"),
        P("group", "head"),
        P("group", "head"),
        P("group", "head"),
        P(),
        P(),
        P("group"),
        P(None, "head"),
        P(None, "head"),
        P("group", "head", None),
        P(),
    )
    out_specs = (P("group", "head"), P("group", "head", None))
    body = functools.partial(shards, mesh.shape["group"], mesh.shape["head"])
    return jax.shard_map(body, mesh=mesh, in_specs=in_specs, out_specs=out_specs, check_vma=False)
```

time: 120 us -> 66.3 us (0.55)
  Pallas kernels: 0 us -> 60.8 us
  blocking collectives: 55.6 us -> 0 us
  waiting for transfers between devices: 25.8 us -> 0 us
  matrix products: 16.1 us -> 0 us
  between operations: 14.9 us -> 1.29 us
  other arithmetic: 2.52 us -> 0 us
  starting transfers between devices: 1.47 us -> 0 us
    pallas_call x0 -> x1, Pallas kernels: none -> 60.8 us  [shards(): pl.pallas_call(functools.partial(kernel, cfg), out_shape=(jax.ShapeDtypeS...]
    all_gather x2 -> x0, blocking collectives: 55.6 us -> none  [the longest x1 28.5 us: shards(): lax.all_gather(cache_values, 'group', axis=0, tiled=True)]
    all_gather x1 -> x0, waiting for transfers between devices: 25.8 us -> none  [shards(): attended_all = lax.all_gather(attended, 'head', axis=1, tiled=True)]
    dot_general x9 -> x0, matrix products: 16.1 us -> none  [the longest x1 7.66 us: shards(): jnp.dot(attended_all, out_weight, preferred_element_type=jnp.float32)]
    unnamed x22 -> x2, local copies, waits for them, and re-layouts: 1.57 us -> 3.84 us
    reduce_sum x4 -> x0, other arithmetic: 1.84 us -> none  [the longest x2 1.12 us: attend(): total_new = total_old * rescale + jnp.sum(weights, axis=-1)]
    all_gather x2 -> x0, local copies, waits for them, and re-layouts: 1.44 us -> none  [the longest x1 1.16 us: shards(): lax.all_gather(cache_values, 'group', axis=0, tiled=True)]
    ppermute x1 -> x0, starting transfers between devices: 1.43 us -> none  [shifted(): return lax.ppermute(array, axis, pairs)]
  transfers between devices with their start and end apart: 2 -> 0, of which waited for: 1 -> 0; matrix products, arithmetic and copies ran while one was open for 3% -> 0% of each run, Pallas kernels for 0% -> 0%
where the time goes in v1:
time: 66.3 us; the launch traced here: 65.9 us
  Pallas kernels  60.8 us (92%)
  local copies, waits for them, and re-layouts  3.84 us (6%)
  between operations  1.29 us (2%)
    pallas_call x1, Pallas kernels, shards(): pl.pallas_call(functools.partial(kernel, cfg), out_shape=(jax.ShapeDtypeS...  60.8 us
    unnamed x2, local copies, waits for them, and re-layouts  3.84 us

profile of v1, /device:TPU:1, one launch (start us, length us, event | category | flops | bytes accessed | tf_op | source)
XLA Modules:
  0.0 65.9 jit_solution(7065442970696606566)
XLA Ops:
  1.3 60.8 %video_attention.1 = (bf16[256,1536]{1,0:T(8,128)(2,1)}, bf16[384,512]{1,0:T(8,128)(2,1)}) custom-call(bf16[256,768]{1,0:T(8,128)(2,1)} %q_hbm.1, bf16[256,768]{1,0:T(8,128)(2,1)} %kn_hbm.1, bf16[256,768]{1,0:T(8,128)(2,1)} %vn_hbm.1, bf16[64,768]{1,0:T(8,128)(2,1)} %ck_hbm.1, bf16[64,768]{1,0:T(8,128)(2,1)} %cv_hbm.1, s32[8]{0:T(128)} %valid_ref.1, ...), custom_call_target="tpu_custom_call" | custom-call | tf_op jit(solution)/shard_map/video_attention/pallas_call | solution.py:350
  62.1 2.1 %copy.17 = bf16[256,1536]{1,0:T(8,128)(2,1)} copy(bf16[256,1536]{1,0:T(8,128)(2,1)} %get-tuple-element.8) | data formatting | bytes 1572864
  64.2 1.8 %copy.18 = bf16[6,64,512]{2,1,0:T(8,128)(2,1)} copy(bf16[6,64,512]{2,1,0:T(8,128)(2,1)} %bitcast.3) | data formatting | bytes 786432

commit v2 on v1

--- a/solution.py
+++ b/solution.py
@@ -24,7 +24,7 @@
     kv_load, w_load, load, kv_recv, up_send, down_send, y_send,
     att_recv, att_send, halo_send, halo_recv,
 ):
-    groups, pieces, per, ahead, crossing = cfg
+    groups, pieces, per, ahead, skew, reach, crossing = cfg
     lines = groups // 2
     krows = kv.shape[4]
     heads_local = pieces * per
@@ -68,30 +68,33 @@
     diag = jnp.where(y == 0, g - 1, g + 1)
     has_diag = jnp.where(y == 0, has_down, has_up)
 
-    @pl.when(has_up)
-    def _():
-        greet(g + 2, hd)
-
-    @pl.when(has_down)
-    def _():
-        greet(g - 2, hd)
+    met = 3 + has_diag.astype(jnp.int32)
+    for r in range(1, reach + 1):
+        met += (z + r < lines).astype(jnp.int32) + (z >= r).astype(jnp.int32)
+
+        @pl.when(z + r < lines)
+        def _():
+            greet(g + 2 * r, hd)
+
+        @pl.when(z >= r)
+        def _():
+            greet(g - 2 * r, hd)
 
     @pl.when(has_diag)
     def _():
         greet(diag, hd)
 
-    pl.semaphore_wait(
-        barrier, 3 + has_up.astype(jnp.int32) + has_down.astype(jnp.int32) + has_diag.astype(jnp.int32))
-
-    def send_up(p, s):
+    pl.semaphore_wait(barrier, met)
+
+    def send_up(p, s, r):
         return pltpu.make_async_remote_copy(
-            kv.at[p, s], kv.at[p, s], up_send.at[p, s], kv_recv.at[p, s],
-            device_id={"group": g + 2, "head": hd}, device_id_type=MESH)
-
-    def send_down(p, s):
+            kv.at[p, s], kv.at[p, s], up_send.at[p, s, r - 1], kv_recv.at[p, s],
+            device_id={"group": g + 2 * r, "head": hd}, device_id_type=MESH)
+
+    def send_down(p, s, r):
         return pltpu.make_async_remote_copy(
-            kv.at[p, s], kv.at[p, s], down_send.at[p, s], kv_recv.at[p, s],
-            device_id={"group": g - 2, "head": hd}, device_id_type=MESH)
+            kv.at[p, s], kv.at[p, s], down_send.at[p, s, r - 1], kv_recv.at[p, s],
+            device_id={"group": g - 2 * r, "head": hd}, device_id_type=MESH)
 
     def send_y(p, s):
         return pltpu.make_async_remote_copy(
@@ -101,87 +104,102 @@
     def received(p, s):
         send_y(p, s).wait_recv()
 
+    def all_up(p, s, start):
+        for r in range(reach, 0, -1):
+            @pl.when(z + r < lines)
+            def _():
+                copy = send_up(p, s, r)
+                copy.start() if start else copy.wait_send()
+
+    def all_down(p, s, start):
+        for r in range(reach, 0, -1):
+            @pl.when(z >= r)
+            def _():
+                copy = send_down(p, s, r)
+                copy.start() if start else copy.wait_send()
+
     def both_ways(p, s):
-        @pl.when(has_up)
-        def _():
-            send_up(p, s).start()
-
-        @pl.when(has_down)
-        def _():
-            send_down(p, s).start()
-
-    def own_sends(p):
+        all_up(p, s, True)
+        all_down(p, s, True)
+
+    def loaded(p):
         for h in range(p * per, p * per + per):
             kv_copies[2 * h].wait()
             kv_copies[2 * h + 1].wait()
+
+    def own_sends(p):
         if p in crossing:
-            send_y(p, g).start()
             both_ways(p, g)
         else:
+            loaded(p)
             both_ways(p, g)
             send_y(p, g).start()
 
-    def forward(p):
+    def pass_on(p, t, col, cross):
+        @pl.when(z >= t)
+        def _():
+            s = (z - t) * 2 + col
+            received(p, s)
+            if t % reach == 0:
+                all_up(p, s, True)
+
+            if not cross:
+                send_y(p, s).start()
+
+        @pl.when(z + t < lines)
+        def _():
+            s = (z + t) * 2 + col
+            received(p, s)
+            if t % reach == 0:
+                all_down(p, s, True)
+
+            if not cross:
+                send_y(p, s).start()
+
+    last = -(-(lines - 1) // reach) + 1
+
+    def forward(k):
+        for p in range(pieces):
+            hop, rest = divmod(k - p, skew)
+            cross = p in crossing
+            if rest or hop < 1 or hop > last:
+                continue
+            near = range((hop - 1) * reach + 1, min(hop * reach, lines - 1) + 1)
+            far = range((hop - 2) * reach + 1, min((hop - 1) * reach, lines - 1) + 1)
+            if cross and hop == 1:
+                received(p, y_peer)
+                both_ways(p, y_peer)
+            for t in near:
+                pass_on(p, t, y, cross)
+            if cross and hop > 1:
+                for t in far:
+                    pass_on(p, t, 1 - y, cross)
+            if not cross and hop == last:
+                def side(s, _):
+                    received(p, s * 2 + 1 - y)
+                    return 0
+
+                lax.fori_loop(0, lines, side, 0)
+
+    def finish_sends(p):
         cross = p in crossing
-        columns = (y, 1 - y) if cross else (y,)
-        if cross:
-            received(p, y_peer)
-            both_ways(p, y_peer)
-
-        def step(t, _):
-            for col in columns:
+        for t in range(0, lines, reach):
+            for col in ((0, 1) if cross else (y,)):
                 @pl.when(z >= t)
                 def _():
-                    s = (z - t) * 2 + col
-                    received(p, s)
-
-                    @pl.when(has_up)
-                    def _():
-                        send_up(p, s).start()
-
-                    if not cross:
-                        send_y(p, s).start()
+                    all_up(p, (z - t) * 2 + col, False)
 
                 @pl.when(z + t < lines)
                 def _():
-                    s = (z + t) * 2 + col
-                    received(p, s)
-
-                    @pl.when(has_down)
-                    def _():
-                        send_down(p, s).start()
-
-                    if not cross:
-                        send_y(p, s).start()
-            return 0
-
-        lax.fori_loop(1, lines, step, 0)
-        if not cross:
-            def side(s, _):
-                received(p, s * 2 + 1 - y)
-                return 0
-
-            lax.fori_loop(0, lines, side, 0)
-
-    def finish_sends(p):
-        cross = p in crossing
-
-        def one(s, _):
-            for col in ((0, 1) if cross else (y,)):
-                @pl.when(has_up & (s <= z))
-                def _():
-                    send_up(p, s * 2 + col).wait_send()
-
-                @pl.when(has_down & (s >= z))
-                def _():
-                    send_down(p, s * 2 + col).wait_send()
-            if not cross:
-                send_y(p, s * 2 + y).wait_send()
-            return 0
-
-        lax.fori_loop(0, lines, one, 0)
+                    all_down(p, (z + t) * 2 + col, False)
         if cross:
             send_y(p, g).wait_send()
+        else:
+            def one(s, _):
+                send_y(p, s * 2 + y).wait_send()
+                return 0
+
+            lax.fori_loop(0, lines, one, 0)
 
     def att_copy(p, slot, which, peer):
         return pltpu.make_async_remote_copy(
@@ -259,6 +277,9 @@
 
     for p in range(min(ahead, pieces)):
         own_sends(p)
+    for p in crossing:
+        loaded(p)
+        send_y(p, g).start()
 
     w_copies = []
     for p in range(pieces):
@@ -290,15 +311,17 @@
     kn_copy.wait()
     vn_copy.wait()
 
-    for p in range(pieces):
-        if p + ahead < pieces:
-            own_sends(p + ahead)
-        forward(p)
+    for k in range(pieces + skew * last):
+        forward(k)
+        if ahead <= k - skew + ahead < pieces:
+            own_sends(k - skew + ahead)
+        p = k - skew * last
         if p == pieces - 1:
             @pl.when(g < groups - 1)
             def _():
                 halo.start()
-        attend(p)
+        if p >= 0:
+            attend(p)
         if p >= 1:
             relay(p - 1)
         if p >= 2:
@@ -308,11 +331,12 @@
     if pieces >= 2:
         project(pieces - 2)
 
+    relay(pieces - 1)
+
     @pl.when(g > 0)
     def _():
         halo.wait_recv()
 
-    relay(pieces - 1)
     convolve(0, pix)
     project(pieces - 1)
 
@@ -325,6 +349,33 @@
         att_copy(p, hd, 1, x_peer).wait_send()
         att_copy(p, hd, 0, core_peer).wait_send()
         att_copy(p, x_peer, 2, core_peer).wait_send()
+
+
+def hand_over_kernel(mixed, decoded, mixed_out, decoded_out, sems):
+    copies = [
+        pltpu.make_async_copy(mixed, mixed_out, sems.at[0]),
+        pltpu.make_async_copy(decoded, decoded_out, sems.at[1]),
+    ]
+    for c in copies:
+        c.start()
+    for c in copies:
+        c.wait()
+
+
+def hand_over(mixed, decoded):
+    anywhere = pl.BlockSpec(memory_space=pl.ANY)
+    vmem = pl.BlockSpec(memory_space=pltpu.VMEM)
+    return pl.pallas_call(
+        hand_over_kernel,
+        out_shape=(
+            jax.ShapeDtypeStruct(mixed.shape, mixed.dtype),
+            jax.ShapeDtypeStruct(decoded.shape, decoded.dtype),
+        ),
+        in_specs=[vmem, vmem],
+        out_specs=(anywhere, anywhere),
+        scratch_shapes=[pltpu.SemaphoreType.DMA((2,))],
+        name="hand_over",
+    )(mixed, decoded)
 
 
 def shards(
@@ -338,9 +389,10 @@
     features = out_weight.shape[1]
     frames, pixels, channels = latents.shape
     pieces = heads_local if groups <= 8 else 1
+    reach = min(1, groups // 2 - 1)
     per = heads_local // pieces
-    crossing = (0,) if pieces > 1 else ()
-    cfg = (groups, pieces, per, 2, crossing)
+    crossing = ()
+    cfg = (groups, pieces, per, 3, 2, reach, crossing)
     lines = groups // 2
     bf16, f32 = jnp.bfloat16, jnp.float32
     dma = pltpu.SemaphoreType.DMA
@@ -371,8 +423,8 @@
             dma((pieces, n_head)),
             dma((6,)),
             dma((pieces, groups)),
-            dma((pieces, groups)),
-            dma((pieces, groups)),
+            dma((pieces, groups, reach)),
+            dma((pieces, groups, reach)),
             dma((pieces, lines)),
             dma((pieces, n_head)),
             dma((pieces, 3)),
@@ -387,6 +439,7 @@
         valid_rows, finished, levels, gate_table, out_weight,
         latents.reshape(frames * pixels, channels), conv_weight,
     )
+    mixed, decoded = hand_over(mixed, decoded)
     return mixed, decoded.reshape(frames, pixels, channels)
 
 

time: 66.3 us -> 42.6 us (0.64)
  Pallas kernels: 60.8 us -> 41.2 us
  local copies, waits for them, and re-layouts: 3.84 us -> 0 us
    pallas_call x1, Pallas kernels: 60.8 us -> 38.9 us  [shards(): pl.pallas_call(functools.partial(kernel, cfg), out_shape=(jax.ShapeDtypeS...]
    unnamed x2 -> x0, local copies, waits for them, and re-layouts: 3.84 us -> none
    pallas_call x0 -> x1, Pallas kernels: none -> 2.25 us  [hand_over(): pl.pallas_call(hand_over_kernel, out_shape=(jax.ShapeDtypeStruct(mixed.sh...]
where the time goes in v2:
time: 42.6 us; the launch traced here: 42.5 us
  Pallas kernels  41.2 us (97%)
  between operations  1.29 us (3%)
    pallas_call x1, Pallas kernels, shards(): pl.pallas_call(functools.partial(kernel, cfg), out_shape=(jax.ShapeDtypeS...  38.9 us
    pallas_call x1, Pallas kernels, hand_over(): pl.pallas_call(hand_over_kernel, out_shape=(jax.ShapeDtypeStruct(mixed.sh...  2.25 us

profile of v2, /device:TPU:1, one launch (start us, length us, event | category | flops | bytes accessed | tf_op | source)
XLA Modules:
  0.0 42.5 jit_solution(12133402961922907004)
XLA Ops:
  1.3 38.9 %video_attention.1 = (bf16[256,1536]{1,0:T(8,128)(2,1)}, bf16[384,512]{1,0:T(8,128)(2,1)}) custom-call(bf16[256,768]{1,0:T(8,128)(2,1)} %q_hbm.1, bf16[256,768]{1,0:T(8,128)(2,1)} %kn_hbm.1, bf16[256,768]{1,0:T(8,128)(2,1)} %vn_hbm.1, bf16[64,768]{1,0:T(8,128)(2,1)} %ck_hbm.1, bf16[64,768]{1,0:T(8,128)(2,1)} %cv_hbm.1, s32[8]{0:T(128)} %valid_ref.1, ...), custom_call_target="tpu_custom_call" | custom-call | tf_op jit(solution)/shard_map/video_attention/pallas_call | solution.py:402
  40.2 2.3 %hand_over.1 = (bf16[256,1536]{1,0:T(8,128)(2,1)}, bf16[384,512]{1,0:T(8,128)(2,1)}) custom-call(bf16[256,1536]{1,0:T(8,128)(2,1)} %get-tuple-element.6.mixed, bf16[384,512]{1,0:T(8,128)(2,1)} %get-tuple-element.7.decoded), custom_call_target="tpu_custom_call" | custom-call | tf_op jit(solution)/shard_map/hand_over/pallas_call | solution.py:368

commit v3 on v2

--- a/solution.py
+++ b/solution.py
@@ -320,10 +320,10 @@
             @pl.when(g < groups - 1)
             def _():
                 halo.start()
+        if p >= 1:
+            relay(p - 1)
         if p >= 0:
             attend(p)
-        if p >= 1:
-            relay(p - 1)
         if p >= 2:
             project(p - 2)
 

time: 42.6 us -> 50.8 us (1.19)
  Pallas kernels: 41.2 us -> 49.4 us
    pallas_call x1, Pallas kernels: 38.9 us -> 47.1 us  [shards(): pl.pallas_call(functools.partial(kernel, cfg), out_shape=(jax.ShapeDtypeS...]
where the time goes in v3:
time: 50.8 us; the launch traced here: 50.7 us
  Pallas kernels  49.4 us (97%)
  between operations  1.29 us (3%)
    pallas_call x1, Pallas kernels, shards(): pl.pallas_call(functools.partial(kernel, cfg), out_shape=(jax.ShapeDtypeS...  47.1 us
    pallas_call x1, Pallas kernels, hand_over(): pl.pallas_call(hand_over_kernel, out_shape=(jax.ShapeDtypeStruct(mixed.sh...  2.25 us

profile of v3, /device:TPU:1, one launch (start us, length us, event | category | flops | bytes accessed | tf_op | source)
XLA Modules:
  0.0 50.7 jit_solution(13310883129996749453)
XLA Ops:
  1.3 47.1 %video_attention.1 = (bf16[256,1536]{1,0:T(8,128)(2,1)}, bf16[384,512]{1,0:T(8,128)(2,1)}) custom-call(bf16[256,768]{1,0:T(8,128)(2,1)} %q_hbm.1, bf16[256,768]{1,0:T(8,128)(2,1)} %kn_hbm.1, bf16[256,768]{1,0:T(8,128)(2,1)} %vn_hbm.1, bf16[64,768]{1,0:T(8,128)(2,1)} %ck_hbm.1, bf16[64,768]{1,0:T(8,128)(2,1)} %cv_hbm.1, s32[8]{0:T(128)} %valid_ref.1, ...), custom_call_target="tpu_custom_call" | custom-call | tf_op jit(solution)/shard_map/video_attention/pallas_call | solution.py:402
  48.4 2.3 %hand_over.1 = (bf16[256,1536]{1,0:T(8,128)(2,1)}, bf16[384,512]{1,0:T(8,128)(2,1)}) custom-call(bf16[256,1536]{1,0:T(8,128)(2,1)} %get-tuple-element.6.mixed, bf16[384,512]{1,0:T(8,128)(2,1)} %get-tuple-element.7.decoded), custom_call_target="tpu_custom_call" | custom-call | tf_op jit(solution)/shard_map/hand_over/pallas_call | solution.py:368
